TPU v7x, 32 devices: a whole 2x2x4 slice. The times are simulated.
32 devices in a mesh: groups: 2 (over y), dp: 4 (over z), layer: 2 (over x), tensor: 2 (over core).
Axes of the slice: x: 2, y: 2, z: 4, core: 2. Of those that a mesh axis runs over, the one named last changes fastest.
Arguments:
- activations: bfloat16 [2, 1536, 14336], P('layer', ('groups', 'dp'), 'tensor'), parts along dimension 1, may hold values from -6 to 6
- out_grads: bfloat16 [2, 1536, 4096], P('layer', ('groups', 'dp'), 'tensor'), parts along dimension 1, may hold values from -6 to 6
- proj_in: bfloat16 [2, 64, 14336], P('layer', None, 'tensor'), may hold values from -0.046875 to 0.046875
- proj_out: bfloat16 [2, 64, 4096], P('layer', None, 'tensor'), may hold values from -0.09375 to 0.09375
- queries: bfloat16 [2, 256, 4096], P('layer', 'dp'), may hold values from -0.0068359375 to 0.0068359375
- lengths: int32 [16], P('groups'), parts along dimension 0, may hold values from 1 to 192, 768 in all
- owner_slot: int32 [16], P('groups'), parts along dimension 0, may hold values from 0 to 7, each once
- pad_mask: int32 [1536], P(('groups', 'dp')), parts along dimension 0, may hold values 0 or 1
Outputs:
- scores: float32 [16, 256], P(('groups', 'dp'), 'layer'), parts along dimension 0
There are 2 independent parts, one for each index of `groups`. A program takes and returns all parts, laid end to end along the dimension named above; an argument that names none is the same for every part. Nothing has to cross between parts.
Inputs may be any that keep to these rules, and one draw needn't show every extreme that they name: `owner_slot`: every output row is the row of exactly one example. The lengths sum to 768; the longest example has exactly 192 tokens.
All inputs are finite; a program needn't handle non-finite values. No bound on the sum of `pad_mask` on one device may be relied on, other than what follows from the above.
Results may differ from a plain program's by a relative error of at most 0.0051.
Values may be sent and summed in bfloat16 or wider, within the bound.
A program may use at most 64 MiB of HBM per device.

v0:
```python
import jax
import jax.numpy as jnp
from jax import lax
from jax.sharding import PartitionSpec as P


def contract_last(left, right):
    return lax.dot_general(
        left, right, (((1,), (1,)), ((), ())), preferred_element_type=jnp.float32
    )


def spread_scores(local_scores):
    return lax.all_to_all(local_scores, "dp", split_axis=0, concat_axis=1, tiled=True)


def local(activations, out_grads, proj_in, proj_out, queries, lengths, owner_slot, pad_mask):
    tok_rows = activations.shape[1]
    rank_out = proj_out.shape[1]
    example_count = lengths.shape[0]
    inner_side = contract_last(activations[0], proj_in[0])
    outer_side = contract_last(out_grads[0], proj_out[0])
    joined = lax.psum(jnp.concatenate([outer_side, inner_side], axis=1), "tensor")
    grad_side = joined[:, :rank_out].astype(jnp.bfloat16)
    act_side = joined[:, rank_out:].astype(jnp.bfloat16)
    row_start = lax.axis_index("dp") * tok_rows
    positions = row_start + jnp.arange(tok_rows, dtype=jnp.int32)
    example_ends = jnp.cumsum(lengths)
    example_of = jnp.sum((positions[:, None] >= example_ends[None, :]).astype(jnp.int32), axis=1)
    labels = jnp.arange(example_count, dtype=jnp.int32)
    slot_of = jnp.sum(
        jnp.where(example_of[:, None] == labels[None, :], owner_slot[None, :], 0), axis=1
    )
    member = jnp.where(slot_of[:, None] == labels[None, :], pad_mask[:, None], 0).astype(
        jnp.bfloat16
    )
    weighted = (member[:, :, None] * grad_side[:, None, :]).reshape(
        tok_rows, example_count * rank_out
    )
    partial_value = lax.dot_general(
        weighted, act_side, (((0,), (0,)), ((), ())), preferred_element_type=jnp.float32
    )
    partial_value = partial_value.reshape(example_count, -1)
    everyone = lax.psum(partial_value, "dp").astype(jnp.bfloat16)
    scores = spread_scores(contract_last(everyone, queries[0]))
    return lax.psum_scatter(scores, "layer", scatter_dimension=1, tiled=True)


def solution(mesh):
    placed = (
        P("layer", ("groups", "dp"), "tensor"),
        P("layer", ("groups", "dp"), "tensor"),
        P("layer", None, "tensor"),
        P("layer", None, "tensor"),
        P("layer", "dp", None),
        P("groups"),
        P("groups"),
        P(("groups", "dp")),
    )
    return jax.shard_map(
        local, mesh=mesh, in_specs=placed, out_specs=P(("groups", "dp"), "layer"), check_vma=False
    )
```

profile of v0, /device:TPU:0, one launch (start us, length us, event | category | flops | bytes accessed | tf_op | source)
XLA Modules:
  0.0 66.9 jit_solution(10035500347536547203)
XLA Ops:
  6.5 0.0 copy-start
  6.5 0.0 reduce-scatter.4.cloned.1.call-start
  6.6 0.0 copy-start.2
  6.6 1.8 %copy-done = bf16[1,192,7168]{2,1,0:T(8,128)(2,1)S(1)} copy-done((bf16[1,192,7168]{2,1,0:T(8,128)(2,1)S(1)}, bf16[1,192,7168]{2,1,0:T(8,128)(2,1)}, u32[]{:S(2)}) %copy-start) | copy-done | bytes 2752536
  8.4 2.2 %fusion = f32[192,64]{0,1:T(8,128)S(1)} fusion(bf16[1,192,7168]{2,1,0:T(8,128)(2,1)S(1)} %copy-done, bf16[1,64,7168]{2,1,0:T(8,128)(2,1)} %param.10), kind=kOutput, calls=%fused_computation | convolution fusion | flops 176160768 | bytes 3719168 | tf_op jit(solution)/shard_map/dot_general | solution.py:8
  10.6 0.4 fusion.3
  11.0 4.1 %psum.14 = bf16[192,128]{0,1:T(8,128)(2,1)S(1)} all-reduce(f32[192,128]{0,1:T(8,128)S(1)} %pad_maximum_fusion), channel_id=1, replica_groups=mesh['groups'=2,'dp'=4,'layer'=2,'tensor'=2] {'tensor'}, use_global_device_ids=true, to_apply=%region_3.4 | all-reduce | flops 24576 | bytes 147456 | tf_op jit(solution)/shard_map/psum | solution.py:23
  15.2 0.2 reduce-window.8
  15.4 0.1 convert_reduce_fusion
  15.4 0.1 select_reduce_fusion
  15.6 0.2 fusion.8
  15.8 0.1 reshape.82
  15.9 22.6 %all-reduce.1 = bf16[8,4096]{1,0:T(8,128)(2,1)S(1)} all-reduce(f32[8,4096]{1,0:T(8,128)S(1)} %reshape.82), channel_id=1, replica_groups=mesh['groups'=2,'dp'=4,'layer'=2,'tensor'=2] {'dp'}, use_global_device_ids=true, to_apply=%region_4.5 | all-reduce | flops 32768 | bytes 196608 | tf_op jit(solution)/shard_map/psum | solution.py:44
  38.5 0.1 dot_general.17
  38.6 1.3 %fusion.5 = f32[4,2,64]{2,1,0:T(2,128)S(1)} fusion(bf16[4,2,4096]{2,1,0:T(2,128)(2,1)S(1)} %dot_general.17, bf16[1,64,4096]{2,1,0:T(8,128)(2,1)} %param.12), kind=kOutput, calls=%fused_computation.5 | convolution fusion | flops 4194304 | bytes 591872 | tf_op jit(solution)/shard_map/dot_general | solution.py:8
  39.9 0.1 reshape.86
  40.0 7.9 %all_to_all.16 = f32[4,1,128]{2,1,0:T(1,128)S(1)} all-to-all(f32[4,1,128]{2,1,0:T(1,128)S(1)} %reshape.86), channel_id=1, replica_groups=mesh['groups'=2,'dp'=4,'layer'=2,'tensor'=2] {'dp'}, dimensions={0} | all-to-all | bytes 4096 | tf_op jit(solution)/shard_map/all_to_all | solution.py:14
  47.9 0.5 broadcast.39
  48.4 0.7 reduce
  49.0 0.1 reshape.87
  49.1 0.8 %copy.20 = f32[2,4,64]{0,2,1:T(8,128)} copy(f32[2,4,64]{2,0,1:T(2,128)S(1)} %bitcast.29) | data formatting | bytes 4096
  49.9 0.0 reduce-scatter.4.cloned.1.call-update
  49.9 8.6 %reduce-scatter.4.cloned.1.call-done = f32[128,2]{1,0:T(8,128)} async-done(((f32[256,2]{1,0:T(8,128)}), f32[128,2]{1,0:T(8,128)}) %reduce-scatter.4.cloned.1.call-update) | async-done | bytes 1040
  58.5 1.5 %copy.19 = f32[2,128]{1,0:T(2,128)} copy(f32[2,128]{0,1:T(8,128)} %bitcast.28) | data formatting | bytes 2048
  (14 shorter events, 0.1 us)
Async XLA Ops:
  6.5 1.9 %copy-start = (bf16[1,192,7168]{2,1,0:T(8,128)(2,1)S(1)}, bf16[1,192,7168]{2,1,0:T(8,128)(2,1)}, u32[]{:S(2)}) copy-start(bf16[1,192,7168]{2,1,0:T(8,128)(2,1)} %param.8) | copy-start | bytes 8257540
  6.5 4.0 %copy-start.1 = (bf16[1,192,2048]{2,1,0:T(8,128)(2,1)S(1)}, bf16[1,192,2048]{2,1,0:T(8,128)(2,1)}, u32[]{:S(2)}) copy-start(bf16[1,192,2048]{2,1,0:T(8,128)(2,1)} %param.9) | copy-start | bytes 2359300
  6.5 8.6 %copy-start.5 = (s32[8]{0:T(128)S(1)}, s32[8]{0:T(128)}, u32[]{:S(2)}) copy-start(s32[8]{0:T(128)} %param.13) | copy-start | bytes 100
  6.5 8.9 %copy-start.4 = (s32[8]{0:T(128)S(1)}, s32[8]{0:T(128)}, u32[]{:S(2)}) copy-start(s32[8]{0:T(128)} %param.14) | copy-start | bytes 100
  6.5 9.0 %copy-start.3 = (s32[192]{0:T(256)S(1)}, s32[192]{0:T(256)}, u32[]{:S(2)}) copy-start(s32[192]{0:T(256)} %param.15) | copy-start | bytes 2308
  6.5 52.0 %reduce-scatter.4.cloned.1.call-start = ((), (), s32[]{:S(2)}) async-start(), calls=%async_computation.2 | async-start | bytes 196608
  6.6 4.0 %copy-start.2 = (bf16[1,64,2048]{2,1,0:T(8,128)(2,1)S(1)}, bf16[1,64,2048]{2,1,0:T(8,128)(2,1)}, u32[]{:S(2)}) copy-start(bf16[1,64,2048]{2,1,0:T(8,128)(2,1)} %param.11) | copy-start | bytes 786436
Sparse Core Ops, SparseCore 0:
  50.0 8.4 reduce-scatter.3
where the time goes:
time: 67.2 us; the launch traced here: 66.9 us
  blocking collectives  34.6 us (51%)
  between operations  13.5 us (20%)
  waiting for transfers between devices  8.66 us (13%)
  local copies, waits for them, and re-layouts  4.9 us (7%)
  matrix products  4.06 us (6%)
  other arithmetic  1.06 us (2%)
    psum x1, blocking collectives, local(): everyone = lax.psum(partial_value, 'dp').astype(jnp.bfloat16)  22.6 us
    unnamed x2, waiting for transfers between devices  8.66 us
    all_to_all x1, blocking collectives, spread_scores(): lax.all_to_all(local_scores, 'dp', split_axis=0, concat_axis=1, tiled=True)  7.88 us
    unnamed x16, local copies, waits for them, and re-layouts  4.21 us
    psum x1, blocking collectives, local(): lax.psum(jnp.concatenate([outer_side, inner_side], axis=1), 'tensor')  4.14 us
    dot_general x3, matrix products, contract_last(): lax.dot_general(left, right, (((1,), (1,)), ((), ())), preferred_element_...  3.85 us
  transfers between devices with their start and end apart: 1, of which 1 were waited for; matrix products, arithmetic and copies ran while one was open for 0% of the time, Pallas kernels for 0%

commit v1 on v0

v1 whole, which is shorter than its diff:
```python
import functools
import jax
import jax.numpy as jnp
from jax import lax
from jax.experimental import pallas as pl
from jax.experimental.pallas import tpu as pltpu
from jax.sharding import PartitionSpec as P

F32 = jnp.float32
BF16 = jnp.bfloat16
NT = (((1,), (1,)), ((), ()))
MESH = pl.DeviceIdType.MESH


def chunks_of(width, most):
    count = most
    while width % (count * 128):
        count -= 1
    return count


def kernel(
    sizes, acts_hbm, grads_hbm, pin_hbm, pout_hbm, query_hbm, len_hbm, own_hbm, pad_hbm, out_ref,
    acts, grads, pin, pout, query, len_s, own_s, pad,
    pair_out, pair_in, gath, gt_ref, acc, sk, sbuf, fin,
    load_sem, pair_send, pair_recv, dp_send, dp_recv, fin_send, fin_recv,
):
    n_dp, n_layer, n_core = sizes
    q, l, c = lax.axis_index("dp"), lax.axis_index("layer"), lax.axis_index("tensor")
    tok = acts.shape[0]
    part = tok // n_core
    r_in, r_out = pin.shape[0], pout.shape[0]
    examples = own_s.shape[0]
    rows, q_out = out_ref.shape
    q_blk = query.shape[0]
    ratio = q_out // q_blk
    ff_chunks = chunks_of(acts.shape[1], 2)
    ff_cut = acts.shape[1] // ff_chunks

    loads = []

    def load(src, dst):
        copy = pltpu.make_async_copy(src, dst, load_sem.at[len(loads)])
        copy.start()
        loads.append(copy)
        return copy

    def token_rows(cc):
        owner = lax.rem(c + cc, n_core)
        return pl.ds(pl.multiple_of(owner * part, part), part)

    order = list(range(1, n_core)) + [0]
    pout_load = load(pout_hbm.at[0], pout)
    side_loads = {}
    pin_loads = {}
    for place, cc in enumerate(order):
        here = token_rows(cc)
        side_loads[cc, "g"] = load(grads_hbm.at[0, here, :], grads.at[here, :])
        for k in range(ff_chunks):
            cols = pl.ds(k * ff_cut, ff_cut)
            if place == 0:
                pin_loads[k] = load(pin_hbm.at[0, :, cols], pin.at[:, cols])
            side_loads[cc, k] = load(acts_hbm.at[0, here, cols], acts.at[here, cols])
    len_load = load(len_hbm, len_s)
    own_load = load(own_hbm, own_s)
    pad_load = load(pad_hbm, pad)
    query_load = load(query_hbm.at[0], query)

    barrier = pltpu.get_barrier_semaphore()
    at_home = q // ratio == l
    for cc in range(1, n_core):
        pl.semaphore_signal(
            barrier, 1, device_id={"tensor": lax.rem(c + cc, n_core)}, device_id_type=MESH
        )
    for k in range(1, n_dp):
        pl.semaphore_signal(
            barrier, 1, device_id={"dp": lax.rem(q + k, n_dp)}, device_id_type=MESH
        )

    def source(rr, ll, cc):
        return (
            l * ratio + lax.rem(q + rr, ratio),
            lax.rem(l + ll, n_layer),
            lax.rem(c + cc, n_core),
        )

    def greet(rr, ll, cc):
        sq, sl, sc = source(rr, ll, cc)
        pl.semaphore_signal(
            barrier, 1, device_id={"dp": sq, "layer": sl, "tensor": sc}, device_id_type=MESH
        )

    for rr in range(ratio):
        for ll in range(n_layer):
            for cc in range(n_core):
                if rr == ll == cc == 0:
                    pl.when(jnp.logical_not(at_home))(functools.partial(greet, rr, ll, cc))
                else:
                    greet(rr, ll, cc)

    def project(cc):
        here = token_rows(cc)
        if cc == order[0]:
            pout_load.wait()
        side_loads[cc, "g"].wait()
        g = lax.dot_general(grads[here, :], pout[...], NT, preferred_element_type=F32)
        a = None
        for k in range(ff_chunks):
            cols = pl.ds(k * ff_cut, ff_cut)
            if cc == order[0]:
                pin_loads[k].wait()
            side_loads[cc, k].wait()
            term = lax.dot_general(acts[here, cols], pin[:, cols], NT, preferred_element_type=F32)
            a = term if a is None else a + term
        return jnp.concatenate([g, a], axis=1)

    pair_copies = []
    for cc in order[:-1]:
        pair_out[cc - 1] = project(cc)
        if cc == order[0]:
            everyone = n_core - 1 + n_dp - 1 + n_dp * n_core
            pl.semaphore_wait(barrier, everyone - at_home.astype(jnp.int32))
        copy = pltpu.make_async_remote_copy(
            src_ref=pair_out.at[cc - 1],
            dst_ref=pair_in.at[cc - 1],
            send_sem=pair_send.at[cc - 1],
            recv_sem=pair_recv.at[cc - 1],
            device_id={"tensor": lax.rem(c + cc, n_core)},
            device_id_type=MESH,
        )
        copy.start()
        pair_copies.append(copy)
    mine = project(0)

    pad_load.wait()
    wide = tok
    mark = (
        lax.broadcasted_iota(jnp.int32, (part, wide), 0) + c * part
        == lax.broadcasted_iota(jnp.int32, (part, wide), 1)
    )
    column = jnp.sum(
        jnp.where(mark, jnp.broadcast_to(pad[...], (part, wide)).astype(F32), 0.0),
        axis=1, keepdims=True,
    )
    lane = lax.broadcasted_iota(jnp.int32, (part, r_out + r_in), 1)
    keep = jnp.where(lane < r_out, column, 1.0)

    for copy in pair_copies:
        copy.wait_recv()
    for cc in range(1, n_core):
        mine = mine + pair_in[cc - 1]
    gath[q] = (mine * keep).astype(BF16)

    hops = sorted(range(1, n_dp), key=lambda k: (abs(k - n_dp / 2), k))
    dp_copies = {}
    for k in hops:
        dp_copies[k] = pltpu.make_async_remote_copy(
            src_ref=gath.at[q],
            dst_ref=gath.at[q],
            send_sem=dp_send.at[k - 1],
            recv_sem=dp_recv.at[k - 1],
            device_id={"dp": lax.rem(q + k, n_dp)},
            device_id_type=MESH,
        )
        dp_copies[k].start()

    len_load.wait()
    own_load.wait()
    bounds = []
    start = jnp.int32(0)
    for e in range(examples):
        end = start + len_s[e]
        bounds.append((start, end, own_s[e]))
        start = end
    label = lax.broadcasted_iota(jnp.int32, (examples, part), 0)
    step_lane = lax.broadcasted_iota(jnp.int32, (examples, part), 1)

    block = max(1, 512 // examples)
    block = min(block, r_out)

    def gather_block(src, first):
        position = step_lane + (src * tok + c * part)
        slot = jnp.full((examples, part), -1, jnp.int32)
        for low, high, owner in bounds:
            inside = (position >= low) & (position < high)
            slot = jnp.where(inside, owner, slot)
        member = jnp.where(slot == label, 1.0, 0.0).astype(F32)
        both = gath[src].astype(F32)
        gt_ref[...] = both.T[:r_out]
        side = both[:, r_out:]
        reps = 128 // r_in
        side = jnp.concatenate([side] * reps, axis=1).astype(BF16)
        for b in range(r_out // block):
            weighted = jnp.concatenate(
                [
                    jnp.broadcast_to(gt_ref[pl.ds(b * block + i, 1), :], (examples, part)) * member
                    for i in range(block)
                ],
                axis=0,
            ).astype(BF16)
            term = jnp.dot(weighted, side, preferred_element_type=F32)
            where = pl.ds(b * block * examples, block * examples)
            if first:
                acc[where, :] = term
            else:
                acc[where, :] += term

    gather_block(q, True)
    for k in hops:
        dp_copies[k].wait_recv()
        gather_block(lax.rem(q + n_dp - k, n_dp), False)

    reps = 128 // r_in
    lanes = lax.broadcasted_iota(jnp.int32, (examples, 128), 1) // r_in
    for t in range(r_out // reps):
        tile = acc[pl.ds(t * reps * examples, examples), :]
        for j in range(1, reps):
            other = acc[pl.ds((t * reps + j) * examples, examples), :]
            tile = jnp.where(lanes == j, other, tile)
        sk[:, pl.ds(t * 128, 128)] = tile.astype(BF16)

    query_load.wait()
    scores = lax.dot_general(sk[...], query[...], NT, preferred_element_type=F32)
    spread = jnp.concatenate([scores] * ratio, axis=1)
    spot = lax.broadcasted_iota(jnp.int32, (examples, q_out), 1) // q_blk
    spread = jnp.where(spot == lax.rem(q, ratio), spread, 0.0)
    for d in range(n_dp):
        sbuf[d] = spread[d * rows:(d + 1) * rows]

    def slot_at(sq, sl, sc):
        return (lax.rem(sq, ratio) * n_layer + sl) * n_core + sc

    my_slot = slot_at(q, l, c)

    def final_copy(dd, cc):
        d = lax.rem(q + dd, n_dp)
        return pltpu.make_async_remote_copy(
            src_ref=sbuf.at[d],
            dst_ref=fin.at[my_slot],
            send_sem=fin_send.at[dd * n_core + cc],
            recv_sem=fin_recv.at[my_slot],
            device_id={"dp": d, "layer": q // ratio, "tensor": lax.rem(c + cc, n_core)},
            device_id_type=MESH,
        )

    for dd in range(n_dp):
        for cc in range(n_core):
            if dd == cc == 0:
                @pl.when(at_home)
                def _():
                    fin[my_slot] = sbuf[q]

                @pl.when(jnp.logical_not(at_home))
                def _():
                    final_copy(0, 0).start()
            else:
                final_copy(dd, cc).start()

    def arrived(rr, ll, cc):
        slot = slot_at(*source(rr, ll, cc))
        pltpu.make_async_remote_copy(
            src_ref=sbuf.at[0],
            dst_ref=fin.at[slot],
            send_sem=fin_send.at[0],
            recv_sem=fin_recv.at[slot],
            device_id={"tensor": lax.rem(c + 1, n_core)},
            device_id_type=MESH,
        ).wait_recv()

    for rr in range(ratio):
        for ll in range(n_layer):
            for cc in range(n_core):
                if rr == ll == cc == 0:
                    pl.when(jnp.logical_not(at_home))(functools.partial(arrived, rr, ll, cc))
                else:
                    arrived(rr, ll, cc)
    total = fin[0]
    for s in range(1, fin.shape[0]):
        total = total + fin[s]
    out_ref[...] = total

    for copy in pair_copies:
        copy.wait_send()
    for k in hops:
        dp_copies[k].wait_send()
    for dd in range(n_dp):
        for cc in range(n_core):
            if dd == cc == 0:
                @pl.when(jnp.logical_not(at_home))
                def _():
                    final_copy(0, 0).wait_send()
            else:
                final_copy(dd, cc).wait_send()


def local(sizes, activations, out_grads, proj_in, proj_out, queries, lengths, owner_slot, pad_mask):
    n_dp, n_layer, n_core = sizes
    tok = activations.shape[1]
    part = tok // n_core
    r_in, r_out = proj_in.shape[1], proj_out.shape[1]
    examples = lengths.shape[0]
    rows = examples // n_dp
    q_blk = queries.shape[1]
    q_out = q_blk * n_dp // n_layer
    sources = n_dp * n_core
    any_spec = pl.BlockSpec(memory_space=pltpu.HBM)
    return pl.pallas_call(
        functools.partial(kernel, sizes),
        out_shape=jax.ShapeDtypeStruct((rows, q_out), F32),
        in_specs=[any_spec] * 8,
        out_specs=pl.BlockSpec(memory_space=pltpu.VMEM),
        scratch_shapes=[
            pltpu.VMEM(activations.shape[1:], BF16),
            pltpu.VMEM(out_grads.shape[1:], BF16),
            pltpu.VMEM(proj_in.shape[1:], BF16),
            pltpu.VMEM(proj_out.shape[1:], BF16),
            pltpu.VMEM(queries.shape[1:], BF16),
            pltpu.SMEM((examples,), jnp.int32),
            pltpu.SMEM((examples,), jnp.int32),
            pltpu.VMEM((1, tok), jnp.int32),
            pltpu.VMEM((n_core - 1, part, r_out + r_in), F32),
            pltpu.VMEM((n_core - 1, part, r_out + r_in), F32),
            pltpu.VMEM((n_dp, part, r_out + r_in), BF16),
            pltpu.VMEM((r_out, part), F32),
            pltpu.VMEM((r_out * examples, 128), F32),
            pltpu.VMEM((examples, r_out * r_in), BF16),
            pltpu.VMEM((n_dp, rows, q_out), F32),
            pltpu.VMEM((sources, rows, q_out), F32),
            pltpu.SemaphoreType.DMA((32,)),
            pltpu.SemaphoreType.DMA((n_core - 1,)),
            pltpu.SemaphoreType.DMA((n_core - 1,)),
            pltpu.SemaphoreType.DMA((n_dp - 1,)),
            pltpu.SemaphoreType.DMA((n_dp - 1,)),
            pltpu.SemaphoreType.DMA((sources,)),
            pltpu.SemaphoreType.DMA((sources,)),
        ],
        compiler_params=pltpu.CompilerParams(
            collective_id=0, has_side_effects=True, vmem_limit_bytes=63 * 1024 * 1024
        ),
    )(
        activations, out_grads, proj_in, proj_out, queries, lengths, owner_slot,
        pad_mask.reshape(1, tok),
    )


def solution(mesh):
    sizes = (mesh.shape["dp"], mesh.shape["layer"], mesh.shape["tensor"])
    placed = (
        P("layer", ("groups", "dp"), "tensor"),
        P("layer", ("groups", "dp"), "tensor"),
        P("layer", None, "tensor"),
        P("layer", None, "tensor"),
        P("layer", "dp", None),
        P("groups"),
        P("groups"),
        P(("groups", "dp")),
    )
    return jax.shard_map(
        functools.partial(local, sizes), mesh=mesh, in_specs=placed,
        out_specs=P(("groups", "dp"), "layer"), check_vma=False,
    )
```

time: 67.2 us -> 17.7 us (0.26)
  blocking collectives: 34.6 us -> 0 us
  Pallas kernels: 0 us -> 16.3 us
  between operations: 13.5 us -> 0.01 us
  waiting for transfers between devices: 8.66 us -> 0 us
  matrix products: 4.06 us -> 0 us
  local copies, waits for them, and re-layouts: 4.9 us -> 1.24 us
  other arithmetic: 1.06 us -> 0 us
    psum x2 -> x0, blocking collectives: 26.7 us -> none  [the longest x1 22.6 us: local(): everyone = lax.psum(partial_value, 'dp').astype(jnp.bfloat16)]
    pallas_call x0 -> x1, Pallas kernels: none -> 16.3 us  [local(): pl.pallas_call(functools.partial(kernel, sizes), out_shape=jax.ShapeDtype...]
    unnamed x2 -> x0, waiting for transfers between devices: 8.66 us -> none
    all_to_all x1 -> x0, blocking collectives: 7.88 us -> none  [spread_scores(): lax.all_to_all(local_scores, 'dp', split_axis=0, concat_axis=1, tiled=True)]
    dot_general x4 -> x0, matrix products: 4.06 us -> none  [the longest x3 3.85 us: contract_last(): lax.dot_general(left, right, (((1,), (1,)), ((), ())), preferred_element_...]
    unnamed x16 -> x1, local copies, waits for them, and re-layouts: 4.21 us -> 1.24 us
  transfers between devices with their start and end apart: 1 -> 0, of which waited for: 1 -> 0; matrix products, arithmetic and copies ran while one was open for 0% -> 0% of each run, Pallas kernels for 0% -> 0%
where the time goes in v1:
time: 17.7 us; the launch traced here: 17.6 us
  Pallas kernels  16.3 us (92%)
  local copies, waits for them, and re-layouts  1.24 us (7%)
    pallas_call x1, Pallas kernels, local(): pl.pallas_call(functools.partial(kernel, sizes), out_shape=jax.ShapeDtype...  16.3 us
    unnamed x1, local copies, waits for them, and re-layouts  1.24 us

profile of v1, /device:TPU:0, one launch (start us, length us, event | category | flops | bytes accessed | tf_op | source)
XLA Modules:
  0.0 17.6 jit_solution(16814831924803443)
XLA Ops:
  0.0 16.3 %shard_map.82 = f32[2,128]{1,0:T(2,128)} custom-call(bf16[1,192,7168]{2,1,0:T(8,128)(2,1)} %acts_hbm.1, bf16[1,192,2048]{2,1,0:T(8,128)(2,1)} %grads_hbm.1, bf16[1,64,7168]{2,1,0:T(8,128)(2,1)} %pin_hbm.1, bf16[1,64,2048]{2,1,0:T(8,128)(2,1)} %pout_hbm.1, bf16[1,64,4096]{2,1,0:T(8,128)(2,1)} %query_hbm.1, s32[8]{0:T(128)} %len_hbm.1, s32[8]{0:T(128)} %own_hbm.1, ...), custom_call_target="tpu_custom_call" | custom-call | tf_op jit(solution)/shard_map/pallas_call | solution.py:307
  16.3 1.2 %copy.10 = f32[2,128]{1,0:T(2,128)} copy(f32[2,128]{1,0:T(2,128)} %shard_map.82) | data formatting | bytes 2048

commit v2 on v1

--- a/solution.py
+++ b/solution.py
@@ -37,6 +37,38 @@
     ff_chunks = chunks_of(acts.shape[1], 2)
     ff_cut = acts.shape[1] // ff_chunks
 
+    barrier = pltpu.get_barrier_semaphore()
+    at_home = q // ratio == l
+    for cc in range(1, n_core):
+        pl.semaphore_signal(
+            barrier, 1, device_id={"tensor": lax.rem(c + cc, n_core)}, device_id_type=MESH
+        )
+    for k in range(1, n_dp):
+        pl.semaphore_signal(
+            barrier, 1, device_id={"dp": lax.rem(q + k, n_dp)}, device_id_type=MESH
+        )
+
+    def source(rr, ll, cc):
+        return (
+            l * ratio + lax.rem(q + rr, ratio),
+            lax.rem(l + ll, n_layer),
+            lax.rem(c + cc, n_core),
+        )
+
+    def greet(rr, ll, cc):
+        sq, sl, sc = source(rr, ll, cc)
+        pl.semaphore_signal(
+            barrier, 1, device_id={"dp": sq, "layer": sl, "tensor": sc}, device_id_type=MESH
+        )
+
+    for rr in range(ratio):
+        for ll in range(n_layer):
+            for cc in range(n_core):
+                if rr == ll == cc == 0:
+                    pl.when(jnp.logical_not(at_home))(functools.partial(greet, rr, ll, cc))
+                else:
+                    greet(rr, ll, cc)
+
     loads = []
 
     def load(src, dst):
@@ -65,38 +97,6 @@
     own_load = load(own_hbm, own_s)
     pad_load = load(pad_hbm, pad)
     query_load = load(query_hbm.at[0], query)
-
-    barrier = pltpu.get_barrier_semaphore()
-    at_home = q // ratio == l
-    for cc in range(1, n_core):
-        pl.semaphore_signal(
-            barrier, 1, device_id={"tensor": lax.rem(c + cc, n_core)}, device_id_type=MESH
-        )
-    for k in range(1, n_dp):
-        pl.semaphore_signal(
-            barrier, 1, device_id={"dp": lax.rem(q + k, n_dp)}, device_id_type=MESH
-        )
-
-    def source(rr, ll, cc):
-        return (
-            l * ratio + lax.rem(q + rr, ratio),
-            lax.rem(l + ll, n_layer),
-            lax.rem(c + cc, n_core),
-        )
-
-    def greet(rr, ll, cc):
-        sq, sl, sc = source(rr, ll, cc)
-        pl.semaphore_signal(
-            barrier, 1, device_id={"dp": sq, "layer": sl, "tensor": sc}, device_id_type=MESH
-        )
-
-    for rr in range(ratio):
-        for ll in range(n_layer):
-            for cc in range(n_core):
-                if rr == ll == cc == 0:
-                    pl.when(jnp.logical_not(at_home))(functools.partial(greet, rr, ll, cc))
-                else:
-                    greet(rr, ll, cc)
 
     def project(cc):
         here = token_rows(cc)
@@ -306,7 +306,7 @@
     any_spec = pl.BlockSpec(memory_space=pltpu.HBM)
     return pl.pallas_call(
         functools.partial(kernel, sizes),
-        out_shape=jax.ShapeDtypeStruct((rows, q_out), F32),
+        out_shape=pltpu.VMEM((rows, q_out), F32),
         in_specs=[any_spec] * 8,
         out_specs=pl.BlockSpec(memory_space=pltpu.VMEM),
         scratch_shapes=[

time: 17.7 us -> 16.5 us (0.932)
  local copies, waits for them, and re-layouts: 1.24 us -> 0.56 us
  Pallas kernels: 16.3 us -> 15.8 us
    unnamed x1, local copies, waits for them, and re-layouts: 1.24 us -> 0.56 us
    pallas_call x1, Pallas kernels: 16.3 us -> 15.8 us  [local(): pl.pallas_call(functools.partial(kernel, sizes), out_shape=pltpu.VMEM((ro...]
where the time goes in v2:
time: 16.5 us; the launch traced here: 16.3 us
  Pallas kernels  15.8 us (96%)
  local copies, waits for them, and re-layouts  0.56 us (3%)
    pallas_call x1, Pallas kernels, local(): pl.pallas_call(functools.partial(kernel, sizes), out_shape=pltpu.VMEM((ro...  15.8 us
    unnamed x1, local copies, waits for them, and re-layouts  0.56 us

profile of v2, /device:TPU:0, one launch (start us, length us, event | category | flops | bytes accessed | tf_op | source)
XLA Modules:
  0.0 16.3 jit_solution(8147790824737449103)
XLA Ops:
  0.0 15.8 %shard_map.82 = f32[2,128]{1,0:T(2,128)S(1)} custom-call(bf16[1,192,7168]{2,1,0:T(8,128)(2,1)} %acts_hbm.1, bf16[1,192,2048]{2,1,0:T(8,128)(2,1)} %grads_hbm.1, bf16[1,64,7168]{2,1,0:T(8,128)(2,1)} %pin_hbm.1, bf16[1,64,2048]{2,1,0:T(8,128)(2,1)} %pout_hbm.1, bf16[1,64,4096]{2,1,0:T(8,128)(2,1)} %query_hbm.1, s32[8]{0:T(128)} %len_hbm.1, s32[8]{0:T(128)} %own_hbm.1, ...), custom_call_target="tpu_custom_call" | custom-call | tf_op jit(solution)/shard_map/pallas_call | solution.py:307
  15.8 0.6 %copy.10 = f32[2,128]{1,0:T(2,128)} copy(f32[2,128]{1,0:T(2,128)S(1)} %shard_map.82) | data formatting | bytes 2048

commit v3 on v2

--- a/solution.py
+++ b/solution.py
@@ -34,7 +34,7 @@
     rows, q_out = out_ref.shape
     q_blk = query.shape[0]
     ratio = q_out // q_blk
-    ff_chunks = chunks_of(acts.shape[1], 2)
+    ff_chunks = chunks_of(acts.shape[1], 4)
     ff_cut = acts.shape[1] // ff_chunks
 
     barrier = pltpu.get_barrier_semaphore()
@@ -82,6 +82,9 @@
         return pl.ds(pl.multiple_of(owner * part, part), part)
 
     order = list(range(1, n_core)) + [0]
+    len_load = load(len_hbm, len_s)
+    own_load = load(own_hbm, own_s)
+    pad_load = load(pad_hbm, pad)
     pout_load = load(pout_hbm.at[0], pout)
     side_loads = {}
     pin_loads = {}
@@ -93,9 +96,6 @@
             if place == 0:
                 pin_loads[k] = load(pin_hbm.at[0, :, cols], pin.at[:, cols])
             side_loads[cc, k] = load(acts_hbm.at[0, here, cols], acts.at[here, cols])
-    len_load = load(len_hbm, len_s)
-    own_load = load(own_hbm, own_s)
-    pad_load = load(pad_hbm, pad)
     query_load = load(query_hbm.at[0], query)
 
     def project(cc):
@@ -114,6 +114,19 @@
             a = term if a is None else a + term
         return jnp.concatenate([g, a], axis=1)
 
+    pad_load.wait()
+    wide = tok
+    mark = (
+        lax.broadcasted_iota(jnp.int32, (part, wide), 0) + c * part
+        == lax.broadcasted_iota(jnp.int32, (part, wide), 1)
+    )
+    column = jnp.sum(
+        jnp.where(mark, jnp.broadcast_to(pad[...], (part, wide)).astype(F32), 0.0),
+        axis=1, keepdims=True,
+    )
+    lane = lax.broadcasted_iota(jnp.int32, (part, r_out + r_in), 1)
+    keep = jnp.where(lane < r_out, column, 1.0)
+
     pair_copies = []
     for cc in order[:-1]:
         pair_out[cc - 1] = project(cc)
@@ -131,19 +144,6 @@
         copy.start()
         pair_copies.append(copy)
     mine = project(0)
-
-    pad_load.wait()
-    wide = tok
-    mark = (
-        lax.broadcasted_iota(jnp.int32, (part, wide), 0) + c * part
-        == lax.broadcasted_iota(jnp.int32, (part, wide), 1)
-    )
-    column = jnp.sum(
-        jnp.where(mark, jnp.broadcast_to(pad[...], (part, wide)).astype(F32), 0.0),
-        axis=1, keepdims=True,
-    )
-    lane = lax.broadcasted_iota(jnp.int32, (part, r_out + r_in), 1)
-    keep = jnp.where(lane < r_out, column, 1.0)
 
     for copy in pair_copies:
         copy.wait_recv()
@@ -232,8 +232,14 @@
 
     my_slot = slot_at(q, l, c)
 
+    def far_first(j):
+        down = n_dp - 1 - j
+        down = jnp.where(down <= q, down - 1, down)
+        up = jnp.where(j >= q, j + 1, j)
+        return jnp.where(q < n_dp // 2, down, up)
+
     def final_copy(dd, cc):
-        d = lax.rem(q + dd, n_dp)
+        d = q if dd == 0 else far_first(dd - 1)
         return pltpu.make_async_remote_copy(
             src_ref=sbuf.at[d],
             dst_ref=fin.at[my_slot],
@@ -243,7 +249,7 @@
             device_id_type=MESH,
         )
 
-    for dd in range(n_dp):
+    for dd in list(range(1, n_dp)) + [0]:
         for cc in range(n_core):
             if dd == cc == 0:
                 @pl.when(at_home)

time: 16.5 us -> 16.1 us (0.976)
  Pallas kernels: 15.8 us -> 15.4 us
    pallas_call x1, Pallas kernels: 15.8 us -> 15.4 us  [local(): pl.pallas_call(functools.partial(kernel, sizes), out_shape=pltpu.VMEM((ro...]
where the time goes in v3:
time: 16.1 us; the launch traced here: 15.9 us
  Pallas kernels  15.4 us (96%)
  local copies, waits for them, and re-layouts  0.56 us (3%)
    pallas_call x1, Pallas kernels, local(): pl.pallas_call(functools.partial(kernel, sizes), out_shape=pltpu.VMEM((ro...  15.4 us
    unnamed x1, local copies, waits for them, and re-layouts  0.56 us

profile of v3, /device:TPU:0, one launch (start us, length us, event | category | flops | bytes accessed | tf_op | source)
XLA Modules:
  0.0 15.9 jit_solution(12184021040790382541)
XLA Ops:
  0.0 15.4 %shard_map.82 = f32[2,128]{1,0:T(2,128)S(1)} custom-call(bf16[1,192,7168]{2,1,0:T(8,128)(2,1)} %acts_hbm.1, bf16[1,192,2048]{2,1,0:T(8,128)(2,1)} %grads_hbm.1, bf16[1,64,7168]{2,1,0:T(8,128)(2,1)} %pin_hbm.1, bf16[1,64,2048]{2,1,0:T(8,128)(2,1)} %pout_hbm.1, bf16[1,64,4096]{2,1,0:T(8,128)(2,1)} %query_hbm.1, s32[8]{0:T(128)} %len_hbm.1, s32[8]{0:T(128)} %own_hbm.1, ...), custom_call_target="tpu_custom_call" | custom-call | tf_op jit(solution)/shard_map/pallas_call | solution.py:313
  15.4 0.6 %copy.10 = f32[2,128]{1,0:T(2,128)} copy(f32[2,128]{1,0:T(2,128)S(1)} %shard_map.82) | data formatting | bytes 2048
